TPU v7x, 768 devices: a whole 4x8x12 slice. The times are simulated.
768 devices in a mesh: row: 24 (over z, y_lo), col: 32 (over x, y_hi, core).
Axes of the slice: x: 4, y: 8 (y_hi: 4, y_lo: 2; y = y_hi * 2 + y_lo), z: 12, core: 2. Of those that a mesh axis runs over, the one named last changes fastest.
Arguments:
- density_panel: bfloat16 [12288, 98304], P('row', 'col'), may hold values from -6 to 6
- density_pattern: int32 [96, 768], P('row', 'col'), may hold values 0 or 1
- margin_blocks: bfloat16 [24, 1024, 128, 128], P('row', 'col'), may hold values from -0.3125 to 0.3125
- margin_owner: int32 [24, 1024, 1], P('row', 'col'), may hold values from 0 to 31; in each aligned block of 32 rows (0 to 31, 32 to 63, ..., all dimensions but the last counted through in order) at most 2 rows name the same one
- margin_place: int32 [24, 1024], P('row', 'col'), may hold values from 0 to 63
Outputs:
- product_panel: float32 [12288, 8192], P('row', 'col')
Inputs may be any that keep to these rules, and one draw needn't show every extreme that they name: `margin_owner`: among the 32 blocks of one device no owner is named more than 2 times.
All inputs are finite; a program needn't handle non-finite values. No bound on the sum of `density_pattern` on one device may be relied on, other than what follows from the above.
Results may differ from a plain program's by a relative error of at most 0.002.
Values may be sent and summed in bfloat16 or wider, within the bound.
A program may use at most 64 MiB of HBM per device.

v0:
```python
import math

import jax
import jax.numpy as jnp
from jax import lax
from jax.sharding import PartitionSpec as P

KB = 1
CB = 2
CAP = 2
SECTIONS = 3


def passed_along(value, axis, steps):
    count = lax.axis_size(axis)
    pairs = [(source, (source + steps) % count) for source in range(count)]
    return lax.ppermute(value, axis, pairs)


def on_device(density_panel, density_pattern, margin_blocks, margin_owner, margin_place):
    rows_here, inner_here = density_panel.shape
    row_blocks, inner_blocks = density_pattern.shape
    width = margin_blocks.shape[-1]
    stack = margin_blocks.shape[1]
    row_count = lax.axis_size("row")
    col_count = lax.axis_size("col")
    common = math.gcd(row_count, col_count)
    period = row_count * col_count // common
    row_index = lax.axis_index("row")
    col_index = lax.axis_index("col")
    group_width = inner_here // row_count
    gates = density_pattern.astype(jnp.bfloat16)[:, None, :, None]
    masked = (density_panel.reshape(row_blocks, width, inner_blocks, width) * gates).reshape(
        rows_here, inner_here
    )
    owners = margin_owner[0, :, 0]
    places = margin_place[0]
    blocks = margin_blocks[0]
    same_owner = owners[:, None] == owners[None, :]
    earlier = jnp.arange(stack)[:, None] < jnp.arange(stack)[None, :]
    ranking = jnp.sum((same_owner & earlier).astype(jnp.int32), axis=0)
    select = (owners[None, None, :] == jnp.arange(col_count)[:, None, None]) & (
        ranking[None, None, :] == jnp.arange(CAP)[None, :, None]
    )
    outgoing = jnp.einsum(
        "dkn,nxy->dkxy", select.astype(jnp.bfloat16), blocks, preferred_element_type=jnp.float32
    ).astype(jnp.bfloat16)
    targets = jnp.sum(select.astype(jnp.int32) * (places + 1)[None, None, :], axis=2) - 1
    incoming, landing = (
        lax.all_to_all(outgoing, "col", split_axis=0, concat_axis=0, tiled=True),
        lax.all_to_all(targets, "col", split_axis=0, concat_axis=0, tiled=True),
    )
    slot_count = col_count * CAP
    positions = col_count * KB * CB
    onehot = (landing.reshape(1, slot_count) == jnp.arange(positions)[:, None]).astype(jnp.bfloat16)
    dense = jnp.einsum(
        "ps,sxy->pxy",
        onehot,
        incoming.reshape(slot_count, width, width),
        preferred_element_type=jnp.float32,
    ).astype(jnp.bfloat16)
    margin_panel = (
        dense.reshape(col_count * KB, CB, width, width)
        .transpose(0, 2, 1, 3)
        .reshape(col_count * KB * width, CB * width)
    )
    total = jnp.zeros((rows_here, CB * width), jnp.float32)
    held_left = masked
    held_right = margin_panel
    for section in range(SECTIONS):
        if section > 0:
            held_left = passed_along(held_left, "col", -1)
            held_right = passed_along(held_right, "row", -1)
        turn = row_index + col_index + section
        base = turn % period
        first_left = (base - turn % col_count) // col_count
        first_right = (base - turn % row_count) // row_count
        left_view = held_left.reshape(rows_here, common, row_count // common, group_width)
        left = lax.dynamic_index_in_dim(left_view, first_left, 2, keepdims=False).reshape(
            rows_here, common * group_width
        )
        right_view = held_right.reshape(common, col_count // common, group_width, CB * width)
        right = lax.dynamic_index_in_dim(right_view, first_right, 1, keepdims=False).reshape(
            common * group_width, CB * width
        )
        total = total + jnp.dot(left, right, preferred_element_type=jnp.float32)
    return total


def solution(mesh):
    return jax.shard_map(
        on_device,
        mesh=mesh,
        in_specs=(
            P("row", "col"),
            P("row", "col"),
            P("row", "col", None, None),
            P("row", "col", None),
            P("row", "col"),
        ),
        out_specs=P("row", "col"),
        check_vma=False,
    )
```

profile of v0, /device:TPU:6, one launch (start us, length us, event | category | flops | bytes accessed | tf_op | source)
XLA Modules:
  0.0 306.4 jit_solution(884001129359510271)
XLA Ops:
  0.0 0.8 convert_reduce_fusion
  0.8 0.7 iota_compare_fusion.2
  1.5 0.7 add_bitcast_fusion.1
  2.1 0.1 fusion.21
  2.3 0.7 copy.30
  3.0 13.1 %all-to-all-start = ((s32[32,1,2]{2,1,0:T(1,128)}), s32[32,1,2]{2,1,0:T(1,128)S(1)}, u32[]{:S(2)}, u32[]{:S(2)}) async-start(s32[32,1,2]{2,1,0:T(1,128)} %copy.30), calls=%async_computation | async-start | bytes 32768 | tf_op jit(solution)/shard_map/all_to_all | solution.py:51
  16.1 2.1 convolution_convert_fusion
  18.3 2.1 copy.32
  20.4 3.5 %all-to-all-done = s32[32,1,2]{2,1,0:T(1,128)S(1)} async-done(((s32[32,1,2]{2,1,0:T(1,128)}), s32[32,1,2]{2,1,0:T(1,128)S(1)}, u32[]{:S(2)}, u32[]{:S(2)}) %all-to-all-start) | async-done | bytes 288 | tf_op jit(solution)/shard_map/all_to_all | solution.py:51
  23.9 6.3 %all-to-all-start.1 = ((bf16[32,2,128,128]{3,2,1,0:T(8,128)(2,1)}), bf16[32,2,128,128]{3,2,1,0:T(8,128)(2,1)S(1)}, u32[]{:S(2)}, u32[]{:S(2)}) async-start(bf16[32,2,128,128]{3,2,1,0:T(8,128)(2,1)} %copy.32), calls=%async_computation.1 | async-start | bytes 4194304 | tf_op jit(solution)/shard_map/all_to_all | solution.py:50
  30.2 0.0 copy-start.1
  30.2 4.7 %copy.27 = bf16[512,3072]{0,1:T(8,128)(2,1)} copy(bf16[512,3072]{1,0:T(8,128)(2,1)} %param.5) | data formatting | bytes 6291456 | tf_op args[0]
  34.9 0.0 copy-done.1
  34.9 0.1 copy.28
  35.0 0.0 copy-start
  35.0 0.9 mul.34
  35.9 1.0 copy-done
  36.9 2.1 bitcast_multiply_fusion
  39.0 5.5 %collective-permute-start = (bf16[512,3072]{0,1:T(8,128)(2,1)}, bf16[512,3072]{0,1:T(8,128)(2,1)}, u32[]{:S(2)}, u32[]{:S(2)}) collective-permute-start(bf16[512,3072]{0,1:T(8,128)(2,1)} %bitcast_multiply_fusion), channel_id=1, source_target_pairs={{0,31},{1,0},{2,1},{3,2},{4,3},{5,4},{6,5},{7,6},{8,7},{9,8},{10,9... | collective-permute-start | bytes 9437192 | tf_op jit(solution)/shard_map/ppermute | solution.py:17
  44.5 0.5 broadcast.68
  45.0 0.7 reduce.3
  45.7 0.1 eq.83
  45.8 63.6 %all-to-all-done.1 = bf16[32,2,128,128]{3,2,1,0:T(8,128)(2,1)S(1)} async-done(((bf16[32,2,128,128]{3,2,1,0:T(8,128)(2,1)}), bf16[32,2,128,128]{3,2,1,0:T(8,128)(2,1)S(1)}, u32[]{:S(2)}, u32[]{:S(2)}) %all-to-all-start.1) | async-done | bytes 2097184 | tf_op jit(solution)/shard_map/all_to_all | solution.py:50
  109.4 3.1 %fusion.2 = bf16[64,128,128]{2,0,1:T(8,128)(2,1)} fusion(bf16[64,128,128]{2,1,0:T(8,128)(2,1)S(1)} %bitcast.77, s32[64]{0:T(128)S(1)} %eq.83), kind=kOutput, calls=%fused_computation.4 | convolution fusion | flops 135270400 | bytes 4194560 | tf_op jit(solution)/shard_map/ps,sxy->pxy/dot_general | solution.py:56
  112.4 4.0 %copy.34 = bf16[32,2,128,128]{2,0,3,1:T(8,128)(2,1)S(1)} copy(bf16[32,2,128,128]{3,1,0,2:T(2,128)(2,1)} %bitcast.78) | data formatting | bytes 4194304 | tf_op jit(solution)/shard_map/reshape | solution.py:63
  116.4 1.0 copy.56
  117.4 1.9 collective-permute-start.1
  119.3 21.2 %collective-permute-done = bf16[512,3072]{0,1:T(8,128)(2,1)} collective-permute-done((bf16[512,3072]{0,1:T(8,128)(2,1)}, bf16[512,3072]{0,1:T(8,128)(2,1)}, u32[]{:S(2)}, u32[]{:S(2)}) %collective-permute-start) | collective-permute-done | bytes 3145760 | tf_op jit(solution)/shard_map/ppermute | solution.py:17
  140.5 6.8 %collective-permute-start.2 = (bf16[512,3072]{0,1:T(8,128)(2,1)}, bf16[512,3072]{0,1:T(8,128)(2,1)}, u32[]{:S(2)}, u32[]{:S(2)}) collective-permute-start(bf16[512,3072]{0,1:T(8,128)(2,1)} %collective-permute-done), channel_id=1, source_target_pairs={{0,31},{1,0},{2,1},{3,2},{4,3},{5,4},{6,5},{7,6},{8,7},{9,8},{10,9... | collective-permute-start | bytes 9437192 | tf_op jit(solution)/shard_map/ppermute | solution.py:17
  147.3 74.6 %collective-permute-done.1 = bf16[4096,256]{0,1:T(8,128)(2,1)} collective-permute-done((bf16[4096,256]{0,1:T(8,128)(2,1)S(1)}, bf16[4096,256]{0,1:T(8,128)(2,1)}, u32[]{:S(2)}, u32[]{:S(2)}) %collective-permute-start.1) | collective-permute-done | bytes 2097184 | tf_op jit(solution)/shard_map/ppermute | solution.py:17
  222.0 13.3 %collective-permute-start.3 = (bf16[4096,256]{0,1:T(8,128)(2,1)}, bf16[4096,256]{0,1:T(8,128)(2,1)}, u32[]{:S(2)}, u32[]{:S(2)}) collective-permute-start(bf16[4096,256]{0,1:T(8,128)(2,1)} %collective-permute-done.1), channel_id=1, source_target_pairs={{0,736},{32,0},{64,32},{96,64},{128,96},{160,128},{192,160},{224,1... | collective-permute-start | bytes 6291464 | tf_op jit(solution)/shard_map/ppermute | solution.py:17
  235.6 0.1 mul.28
  235.8 1.1 constant_dynamic-slice_fusion
  236.9 0.9 copy.43
  237.8 1.7 convolution_bitcast_fusion.2
  239.5 3.3 %copy.39 = bf16[4096,256]{1,0:T(8,128)(2,1)S(1)} copy(bf16[4096,256]{0,1:T(8,128)(2,1)} %collective-permute-done.1) | data formatting | bytes 4194304 | tf_op jit(solution)/shard_map/ppermute | solution.py:17
  242.8 1.7 fusion.5
  244.5 56.1 %collective-permute-done.3 = bf16[4096,256]{0,1:T(8,128)(2,1)} collective-permute-done((bf16[4096,256]{0,1:T(8,128)(2,1)}, bf16[4096,256]{0,1:T(8,128)(2,1)}, u32[]{:S(2)}, u32[]{:S(2)}) %collective-permute-start.3) | collective-permute-done | bytes 2097184 | tf_op jit(solution)/shard_map/ppermute | solution.py:17
  300.6 3.3 %copy.41 = bf16[4096,256]{1,0:T(8,128)(2,1)S(1)} copy(bf16[4096,256]{0,1:T(8,128)(2,1)} %collective-permute-done.3) | data formatting | bytes 4194304 | tf_op jit(solution)/shard_map/ppermute | solution.py:17
  303.9 0.0 collective-permute-done.2
  303.9 2.5 fusion.6
  (5 shorter events, 0.1 us)
Async XLA Ops:
  3.0 20.9 %all-to-all-start = ((s32[32,1,2]{2,1,0:T(1,128)}), s32[32,1,2]{2,1,0:T(1,128)S(1)}, u32[]{:S(2)}, u32[]{:S(2)}) async-start(s32[32,1,2]{2,1,0:T(1,128)} %copy.30), calls=%async_computation | async-start | bytes 32768 | tf_op jit(solution)/shard_map/all_to_all | solution.py:51
  23.9 85.5 %all-to-all-start.1 = ((bf16[32,2,128,128]{3,2,1,0:T(8,128)(2,1)}), bf16[32,2,128,128]{3,2,1,0:T(8,128)(2,1)S(1)}, u32[]{:S(2)}, u32[]{:S(2)}) async-start(bf16[32,2,128,128]{3,2,1,0:T(8,128)(2,1)} %copy.32), calls=%async_computation.1 | async-start | bytes 4194304 | tf_op jit(solution)/shard_map/all_to_all | solution.py:50
  30.2 4.7 %copy-start.1 = (s32[4,24]{1,0:T(4,128)S(1)}, s32[4,24]{1,0:T(4,128)}, u32[]{:S(2)}) copy-start(s32[4,24]{1,0:T(4,128)} %param.6) | copy-start | bytes 1156
  35.0 1.9 copy-start
  39.0 101.5 %collective-permute-start = (bf16[512,3072]{0,1:T(8,128)(2,1)}, bf16[512,3072]{0,1:T(8,128)(2,1)}, u32[]{:S(2)}, u32[]{:S(2)}) collective-permute-start(bf16[512,3072]{0,1:T(8,128)(2,1)} %bitcast_multiply_fusion), channel_id=1, source_target_pairs={{0,31},{1,0},{2,1},{3,2},{4,3},{5,4},{6,5},{7,6},{8,7},{9,8},{10,9... | collective-permute-start | bytes 9437192 | tf_op jit(solution)/shard_map/ppermute | solution.py:17
  117.4 104.6 %collective-permute-start.1 = (bf16[4096,256]{0,1:T(8,128)(2,1)S(1)}, bf16[4096,256]{0,1:T(8,128)(2,1)}, u32[]{:S(2)}, u32[]{:S(2)}) collective-permute-start(bf16[4096,256]{0,1:T(8,128)(2,1)S(1)} %bitcast.81), channel_id=1, source_target_pairs={{0,736},{32,0},{64,32},{96,64},{128,96},{160,128},{192,160},{224,1... | collective-permute-start | bytes 6291464 | tf_op jit(solution)/shard_map/ppermute | solution.py:17
  140.5 163.4 %collective-permute-start.2 = (bf16[512,3072]{0,1:T(8,128)(2,1)}, bf16[512,3072]{0,1:T(8,128)(2,1)}, u32[]{:S(2)}, u32[]{:S(2)}) collective-permute-start(bf16[512,3072]{0,1:T(8,128)(2,1)} %collective-permute-done), channel_id=1, source_target_pairs={{0,31},{1,0},{2,1},{3,2},{4,3},{5,4},{6,5},{7,6},{8,7},{9,8},{10,9... | collective-permute-start | bytes 9437192 | tf_op jit(solution)/shard_map/ppermute | solution.py:17
  222.0 78.6 %collective-permute-start.3 = (bf16[4096,256]{0,1:T(8,128)(2,1)}, bf16[4096,256]{0,1:T(8,128)(2,1)}, u32[]{:S(2)}, u32[]{:S(2)}) collective-permute-start(bf16[4096,256]{0,1:T(8,128)(2,1)} %collective-permute-done.1), channel_id=1, source_target_pairs={{0,736},{32,0},{64,32},{96,64},{128,96},{160,128},{192,160},{224,1... | collective-permute-start | bytes 6291464 | tf_op jit(solution)/shard_map/ppermute | solution.py:17
where the time goes:
time: 308 us; the launch traced here: 306 us
  waiting for transfers between devices  219 us (71%)
  starting transfers between devices  47 us (15%)
  local copies, waits for them, and re-layouts  23.8 us (8%)
  matrix products  11.1 us (4%)
  other arithmetic  5.06 us (2%)
    ppermute x4, waiting for transfers between devices, passed_along(): return lax.ppermute(value, axis, pairs)  152 us
    all_to_all x1, waiting for transfers between devices, on_device(): lax.all_to_all(outgoing, 'col', split_axis=0, concat_axis=0, tiled=True)  63.6 us
    ppermute x4, starting transfers between devices, passed_along(): return lax.ppermute(value, axis, pairs)  27.6 us
    all_to_all x1, starting transfers between devices, on_device(): lax.all_to_all(targets, 'col', split_axis=0, concat_axis=0, tiled=True)  13.1 us
    unnamed x7, local copies, waits for them, and re-layouts  7.6 us
    ppermute x2, local copies, waits for them, and re-layouts, passed_along(): return lax.ppermute(value, axis, pairs)  6.54 us
    all_to_all x1, starting transfers between devices, on_device(): lax.all_to_all(outgoing, 'col', split_axis=0, concat_axis=0, tiled=True)  6.31 us
  transfers between devices with their start and end apart: 6, of which 5 were waited for; matrix products, arithmetic and copies ran while one was open for 11% of the time, Pallas kernels for 0%

commit v1 on v0

v1 whole, which is shorter than its diff:
```python
import jax
import jax.numpy as jnp
from jax import lax
from jax.sharding import PartitionSpec as P

CB = 2
CAP = 2
SECTIONS = 3
WIDTH = 128


def shifted(value, axis, steps):
    count = lax.axis_size(axis)
    pairs = [(source, (source + steps) % count) for source in range(count)]
    return lax.ppermute(value, axis, pairs)


def on_device(density_panel, density_pattern, margin_blocks, margin_owner, margin_place):
    rows_here, inner_here = density_panel.shape
    row_blocks, inner_blocks = density_pattern.shape
    stack = margin_blocks.shape[1]
    row_count = lax.axis_size("row")
    col_count = lax.axis_size("col")
    row_index = lax.axis_index("row")
    col_index = lax.axis_index("col")
    common = 8
    left_turns = row_count // common
    right_turns = col_count // common
    period = row_count * right_turns

    owners = margin_owner[0, :, 0]
    places = margin_place[0]
    blocks = margin_blocks[0]
    same_owner = owners[:, None] == owners[None, :]
    earlier = jnp.arange(stack)[:, None] < jnp.arange(stack)[None, :]
    ranking = jnp.sum((same_owner & earlier).astype(jnp.int32), axis=0)
    select = (owners[None, None, :] == jnp.arange(col_count)[:, None, None]) & (
        ranking[None, None, :] == jnp.arange(CAP)[None, :, None]
    )
    outgoing = jnp.einsum(
        "dkn,nxy->dkxy", select.astype(jnp.bfloat16), blocks, preferred_element_type=jnp.float32
    ).astype(jnp.bfloat16)
    targets = jnp.sum(select.astype(jnp.int32) * (places + 1)[None, None, :], axis=2) - 1
    incoming = lax.all_to_all(outgoing, "col", split_axis=0, concat_axis=0, tiled=True)
    landing = lax.all_to_all(targets, "col", split_axis=0, concat_axis=0, tiled=True)

    left_view = density_panel.reshape(rows_here, common, left_turns, WIDTH)
    gate_view = density_pattern.reshape(row_blocks, common, left_turns)

    def left_part(section):
        home = lax.rem(col_index + col_count - section, col_count)
        turn = lax.rem(row_index + home + section, period)
        first = turn // col_count
        part = lax.dynamic_index_in_dim(left_view, first, 2, keepdims=False)
        gate = lax.dynamic_index_in_dim(gate_view, first, 2, keepdims=False).astype(jnp.bfloat16)
        part = part.reshape(row_blocks, WIDTH, common, WIDTH) * gate[:, None, :, None]
        return part.reshape(rows_here, common * WIDTH)

    lefts = [left_part(0)] + [shifted(left_part(s), "col", -s) for s in range(1, SECTIONS)]

    slot_count = col_count * CAP
    landing = landing.reshape(slot_count)
    wanted = []
    for section in range(SECTIONS):
        home = lax.rem(row_index + row_count - section, row_count)
        turn = lax.rem(home + col_index + section, period)
        first = turn // row_count
        inner = first + right_turns * jnp.arange(common)
        wanted.append((inner[:, None] * CB + jnp.arange(CB)[None, :]).reshape(-1))
    wanted = jnp.stack(wanted)
    onehot = (landing[None, None, :] == wanted[:, :, None]).astype(jnp.bfloat16)
    dense = jnp.einsum(
        "aps,sxy->apxy",
        onehot,
        incoming.reshape(slot_count, WIDTH, WIDTH),
        preferred_element_type=jnp.float32,
    ).astype(jnp.bfloat16)
    dense = dense.reshape(SECTIONS, common, CB, WIDTH, WIDTH).transpose(0, 1, 3, 2, 4)
    dense = dense.reshape(SECTIONS, common * WIDTH, CB * WIDTH)
    rights = [dense[0]] + [shifted(dense[s], "row", -s) for s in range(1, SECTIONS)]
    total = jnp.dot(lefts[0], rights[0], preferred_element_type=jnp.float32)
    for section in range(1, SECTIONS):
        total = total + jnp.dot(lefts[section], rights[section], preferred_element_type=jnp.float32)
    return total


def solution(mesh):
    return jax.shard_map(
        on_device,
        mesh=mesh,
        in_specs=(
            P("row", "col"),
            P("row", "col"),
            P("row", "col", None, None),
            P("row", "col", None),
            P("row", "col"),
        ),
        out_specs=P("row", "col"),
        check_vma=False,
    )
```

time: 308 us -> 161 us (0.52)
  waiting for transfers between devices: 219 us -> 84.8 us
  local copies, waits for them, and re-layouts: 23.8 us -> 10.1 us
    ppermute x4, waiting for transfers between devices: 152 us -> 22.6 us  [shifted(): return lax.ppermute(value, axis, pairs)]
    ppermute x2 -> x0, local copies, waits for them, and re-layouts: 6.54 us -> none  [passed_along(): return lax.ppermute(value, axis, pairs)]
    all_to_all x1, waiting for transfers between devices: 63.6 us -> 58.7 us  [on_device(): lax.all_to_all(outgoing, 'col', split_axis=0, concat_axis=0, tiled=True)]
    unnamed x7 -> x9, local copies, waits for them, and re-layouts: 7.6 us -> 3.39 us
  transfers between devices with their start and end apart: 6 -> 6, of which waited for: 5 -> 3; matrix products, arithmetic and copies ran while one was open for 11% -> 14% of each run, Pallas kernels for 0% -> 0%
where the time goes in v1:
time: 161 us; the launch traced here: 159 us
  waiting for transfers between devices  84.8 us (53%)
  starting transfers between devices  46 us (29%)
  local copies, waits for them, and re-layouts  10.1 us (6%)
  matrix products  10.1 us (6%)
  other arithmetic  7.48 us (5%)
    all_to_all x1, waiting for transfers between devices, on_device(): lax.all_to_all(outgoing, 'col', split_axis=0, concat_axis=0, tiled=True)  58.7 us
    ppermute x4, starting transfers between devices, shifted(): return lax.ppermute(value, axis, pairs)  26.3 us
    ppermute x4, waiting for transfers between devices, shifted(): return lax.ppermute(value, axis, pairs)  22.6 us
    all_to_all x1, starting transfers between devices, on_device(): lax.all_to_all(targets, 'col', split_axis=0, concat_axis=0, tiled=True)  13.1 us
    all_to_all x1, starting transfers between devices, on_device(): lax.all_to_all(outgoing, 'col', split_axis=0, concat_axis=0, tiled=True)  6.61 us
    dot_general x2, matrix products, on_device(): jnp.dot(lefts[section], rights[section], preferred_element_type=jnp.float32)  4.22 us
    all_to_all x1, waiting for transfers between devices, on_device(): lax.all_to_all(targets, 'col', split_axis=0, concat_axis=0, tiled=True)  3.49 us
    unnamed x9, local copies, waits for them, and re-layouts  3.39 us
  transfers between devices with their start and end apart: 6, of which 3 were waited for; matrix products, arithmetic and copies ran while one was open for 14% of the time, Pallas kernels for 0%

profile of v1, /device:TPU:6, one launch (start us, length us, event | category | flops | bytes accessed | tf_op | source)
XLA Modules:
  0.0 159.0 jit_solution(10345943490470769773)
XLA Ops:
  0.0 0.8 convert_reduce_fusion
  0.8 0.7 iota_compare_fusion.1
  1.5 0.7 add_bitcast_fusion.1
  2.1 0.1 fusion.11
  2.3 0.7 copy.17
  3.0 13.1 %all-to-all-start = ((s32[32,1,2]{2,1,0:T(1,128)}), s32[32,1,2]{2,1,0:T(1,128)S(1)}, u32[]{:S(2)}, u32[]{:S(2)}) async-start(s32[32,1,2]{2,1,0:T(1,128)} %copy.17), calls=%async_computation | async-start | bytes 32768 | tf_op jit(solution)/shard_map/all_to_all | solution.py:45
  16.1 2.1 %convolution_convert_fusion = bf16[32,2,128,128]{3,0,2,1:T(8,128)(2,1)S(1)} fusion(bf16[32,128,128]{2,1,0:T(8,128)(2,1)} %bitcast.82, pred[2,32]{1,0:T(4,128)(4,1)S(1)} %iota_compare_fusion.2, pred[32,32]{1,0:T(8,128)(4,1)S(1)} %iota_compare_fusion.1), kind=kOutput, calls=%fused_computation.3 | convolution fusion | flops 68159488 | bytes 3146816 | tf_op jit(solution)/shard_map/dkn,nxy->dkxy/dot_general | solution.py:40
  18.3 2.1 %copy.19 = bf16[32,2,128,128]{3,2,1,0:T(8,128)(2,1)} copy(bf16[32,2,128,128]{3,0,2,1:T(8,128)(2,1)S(1)} %convolution_convert_fusion) | data formatting | bytes 4194304 | tf_op jit(solution)/shard_map/convert_element_type | solution.py:42
  20.4 3.5 %all-to-all-done = s32[32,1,2]{2,1,0:T(1,128)S(1)} async-done(((s32[32,1,2]{2,1,0:T(1,128)}), s32[32,1,2]{2,1,0:T(1,128)S(1)}, u32[]{:S(2)}, u32[]{:S(2)}) %all-to-all-start) | async-done | bytes 288 | tf_op jit(solution)/shard_map/all_to_all | solution.py:45
  23.9 6.6 %all-to-all-start.1 = ((bf16[32,2,128,128]{3,2,1,0:T(8,128)(2,1)}), bf16[32,2,128,128]{3,2,1,0:T(8,128)(2,1)}, u32[]{:S(2)}, u32[]{:S(2)}) async-start(bf16[32,2,128,128]{3,2,1,0:T(8,128)(2,1)} %copy.19), calls=%async_computation.1 | async-start | bytes 4194304 | tf_op jit(solution)/shard_map/all_to_all | solution.py:44
  30.6 0.0 copy-start.2
  30.6 3.2 %copy.16 = bf16[512,3072]{0,1:T(8,128)(2,1)S(1)} copy(bf16[512,3072]{1,0:T(8,128)(2,1)} %param.5) | data formatting | bytes 6291456 | tf_op args[0]
  33.8 0.1 reshape.215
  33.9 0.1 dynamic-slice_convert_fusion
  34.0 0.2 copy.26
  34.1 0.2 fusion.19
  34.3 0.1 broadcast_bitcast_fusion
  34.4 1.6 constant_dynamic-slice_fusion
  35.9 0.3 mul.100
  36.3 1.3 bitcast_multiply_fusion.1
  37.5 5.5 %collective-permute-start = (bf16[512,1024]{0,1:T(8,128)(2,1)}, bf16[512,1024]{0,1:T(8,128)(2,1)}, u32[]{:S(2)}, u32[]{:S(2)}) collective-permute-start(bf16[512,1024]{0,1:T(8,128)(2,1)} %bitcast_multiply_fusion.1), channel_id=1, source_target_pairs={{0,31},{1,0},{2,1},{3,2},{4,3},{5,4},{6,5},{7,6},{8,7},{9,8},{10,9... | collective-permute-start | bytes 3145736 | tf_op jit(solution)/shard_map/ppermute | solution.py:15
  43.0 0.1 copy.27
  43.2 0.3 mul.103
  43.5 1.2 bitcast_multiply_fusion
  44.8 4.2 %collective-permute-start.2 = (bf16[512,1024]{0,1:T(8,128)(2,1)}, bf16[512,1024]{0,1:T(8,128)(2,1)}, u32[]{:S(2)}, u32[]{:S(2)}) collective-permute-start(bf16[512,1024]{0,1:T(8,128)(2,1)} %bitcast_multiply_fusion), channel_id=1, source_target_pairs={{0,30},{1,31},{2,0},{3,1},{4,2},{5,3},{6,4},{7,5},{8,6},{9,7},{10,... | collective-permute-start | bytes 3145736 | tf_op jit(solution)/shard_map/ppermute | solution.py:15
  49.1 0.1 iota_add_fusion
  49.2 0.1 add.228
  49.3 0.1 iota_add_fusion.1
  49.4 0.1 add.220
  49.5 0.1 iota_add_fusion.2
  49.5 0.1 add.212
  49.6 0.5 broadcast.134
  50.2 0.7 reduce.5
  50.8 0.1 eq.73
  50.9 58.7 %all-to-all-done.1 = bf16[32,2,128,128]{3,2,1,0:T(8,128)(2,1)} async-done(((bf16[32,2,128,128]{3,2,1,0:T(8,128)(2,1)}), bf16[32,2,128,128]{3,2,1,0:T(8,128)(2,1)}, u32[]{:S(2)}, u32[]{:S(2)}) %all-to-all-start.1) | async-done | bytes 2097184 | tf_op jit(solution)/shard_map/all_to_all | solution.py:44
  109.6 3.3 %fusion.3 = bf16[3,16,128,128]{3,1,2,0:T(8,128)(2,1)S(1)} fusion(bf16[64,128,128]{2,1,0:T(8,128)(2,1)} %bitcast.12, s32[3,16]{1,0:T(4,128)S(1)} %pad_add_fusion, s32[64]{0:T(128)S(1)} %eq.73), kind=kOutput, calls=%fused_computation.4 | convolution fusion | flops 101452800 | bytes 3670464 | tf_op jit(solution)/shard_map/aps,sxy->apxy/dot_general | solution.py:72
  112.9 1.8 %copy.21 = bf16[3,8,2,128,128]{3,1,4,2,0:T(8,128)(2,1)S(1)} copy(bf16[3,8,2,128,128]{4,2,1,3,0:T(2,128)(2,1)S(1)} %bitcast.77) | data formatting | bytes 3145728 | tf_op jit(solution)/shard_map/reshape | solution.py:78
  114.7 0.1 fusion.20
  114.8 0.1 copy.52
  114.9 2.1 %collective-permute-start.1 = (bf16[1024,256]{0,1:T(8,128)(2,1)S(1)}, bf16[1024,256]{0,1:T(8,128)(2,1)S(1)}, u32[]{:S(2)}, u32[]{:S(2)}) collective-permute-start(bf16[1024,256]{0,1:T(8,128)(2,1)S(1)} %bitcast.85), channel_id=1, source_target_pairs={{0,736},{32,0},{64,32},{96,64},{128,96},{160,128},{192,160},{224,1... | collective-permute-start | bytes 1572872 | tf_op jit(solution)/shard_map/ppermute | solution.py:15
  117.0 0.1 copy.51
  117.1 14.5 %collective-permute-start.3 = (bf16[1024,256]{0,1:T(8,128)(2,1)S(1)}, bf16[1024,256]{0,1:T(8,128)(2,1)S(1)}, u32[]{:S(2)}, u32[]{:S(2)}) collective-permute-start(bf16[1024,256]{0,1:T(8,128)(2,1)S(1)} %bitcast.84), channel_id=1, source_target_pairs={{0,704},{32,736},{64,0},{96,32},{128,64},{160,96},{192,128},{224,1... | collective-permute-start | bytes 1572872 | tf_op jit(solution)/shard_map/ppermute | solution.py:15
  131.6 0.5 fusion.8
  132.1 0.0 collective-permute-done
  132.1 22.6 %collective-permute-done.1 = bf16[1024,256]{0,1:T(8,128)(2,1)S(1)} collective-permute-done((bf16[1024,256]{0,1:T(8,128)(2,1)S(1)}, bf16[1024,256]{0,1:T(8,128)(2,1)S(1)}, u32[]{:S(2)}, u32[]{:S(2)}) %collective-permute-start.1) | collective-permute-done | bytes 524320 | tf_op jit(solution)/shard_map/ppermute | solution.py:15
  154.7 1.7 %convolution_add_fusion.1 = f32[512,256]{1,0:T(8,128)S(1)} fusion(f32[512,256]{1,0:T(8,128)S(1)} %fusion.8, bf16[512,1024]{0,1:T(8,128)(2,1)} %collective-permute-done, bf16[1024,256]{0,1:T(8,128)(2,1)S(1)} %collective-permute-done.1), kind=kOutput, calls=%fused_computation.6 | convolution fusion | flops 268566528 | bytes 2621440 | tf_op jit(solution)/shard_map/dot_general | solution.py:83
  156.4 0.0 collective-permute-done.2
  156.5 2.5 %convolution_add_fusion = f32[512,256]{1,0:T(8,128)} fusion(f32[512,256]{1,0:T(8,128)S(1)} %convolution_add_fusion.1, bf16[512,1024]{0,1:T(8,128)(2,1)} %collective-permute-done.2, bf16[1024,256]{0,1:T(8,128)(2,1)S(1)} %collective-permute-done.3), kind=kOutput, calls=%fused_computation.5 | convolution fusion | flops 268566528 | bytes 2621440 | tf_op jit(solution)/shard_map/dot_general | solution.py:83
  (12 shorter events, 0.1 us)
Async XLA Ops:
  3.0 20.9 %all-to-all-start = ((s32[32,1,2]{2,1,0:T(1,128)}), s32[32,1,2]{2,1,0:T(1,128)S(1)}, u32[]{:S(2)}, u32[]{:S(2)}) async-start(s32[32,1,2]{2,1,0:T(1,128)} %copy.17), calls=%async_computation | async-start | bytes 32768 | tf_op jit(solution)/shard_map/all_to_all | solution.py:45
  23.9 85.7 %all-to-all-start.1 = ((bf16[32,2,128,128]{3,2,1,0:T(8,128)(2,1)}), bf16[32,2,128,128]{3,2,1,0:T(8,128)(2,1)}, u32[]{:S(2)}, u32[]{:S(2)}) async-start(bf16[32,2,128,128]{3,2,1,0:T(8,128)(2,1)} %copy.19), calls=%async_computation.1 | async-start | bytes 4194304 | tf_op jit(solution)/shard_map/all_to_all | solution.py:44
  30.6 3.2 %copy-start.2 = (s32[4,24]{1,0:T(4,128)S(1)}, s32[4,24]{1,0:T(4,128)}, u32[]{:S(2)}) copy-start(s32[4,24]{1,0:T(4,128)} %param.6) | copy-start | bytes 1156
  36.3 7.3 %copy-start = (bf16[512,8,1,128]{0,3,2,1:T(8,128)(2,1)S(1)}, bf16[512,8,1,128]{0,3,2,1:T(8,128)(2,1)}, u32[]{:S(2)}) copy-start(bf16[512,8,1,128]{0,3,2,1:T(8,128)(2,1)} %get-tuple-element.5) | copy-start | bytes 3145732
  37.5 94.6 %collective-permute-start = (bf16[512,1024]{0,1:T(8,128)(2,1)}, bf16[512,1024]{0,1:T(8,128)(2,1)}, u32[]{:S(2)}, u32[]{:S(2)}) collective-permute-start(bf16[512,1024]{0,1:T(8,128)(2,1)} %bitcast_multiply_fusion.1), channel_id=1, source_target_pairs={{0,31},{1,0},{2,1},{3,2},{4,3},{5,4},{6,5},{7,6},{8,7},{9,8},{10,9... | collective-permute-start | bytes 3145736 | tf_op jit(solution)/shard_map/ppermute | solution.py:15
  44.8 111.7 %collective-permute-start.2 = (bf16[512,1024]{0,1:T(8,128)(2,1)}, bf16[512,1024]{0,1:T(8,128)(2,1)}, u32[]{:S(2)}, u32[]{:S(2)}) collective-permute-start(bf16[512,1024]{0,1:T(8,128)(2,1)} %bitcast_multiply_fusion), channel_id=1, source_target_pairs={{0,30},{1,31},{2,0},{3,1},{4,2},{5,3},{6,4},{7,5},{8,6},{9,7},{10,... | collective-permute-start | bytes 3145736 | tf_op jit(solution)/shard_map/ppermute | solution.py:15
  114.7 16.9 %copy-start.1 = (bf16[512,8,1,128]{0,3,2,1:T(8,128)(2,1)S(1)}, bf16[512,8,1,128]{0,3,2,1:T(8,128)(2,1)}, u32[]{:S(2)}) copy-start(bf16[512,8,1,128]{0,3,2,1:T(8,128)(2,1)} %get-tuple-element.7) | copy-start | bytes 3145732
  114.9 39.8 %collective-permute-start.1 = (bf16[1024,256]{0,1:T(8,128)(2,1)S(1)}, bf16[1024,256]{0,1:T(8,128)(2,1)S(1)}, u32[]{:S(2)}, u32[]{:S(2)}) collective-permute-start(bf16[1024,256]{0,1:T(8,128)(2,1)S(1)} %bitcast.85), channel_id=1, source_target_pairs={{0,736},{32,0},{64,32},{96,64},{128,96},{160,128},{192,160},{224,1... | collective-permute-start | bytes 1572872 | tf_op jit(solution)/shard_map/ppermute | solution.py:15
  117.1 39.3 %collective-permute-start.3 = (bf16[1024,256]{0,1:T(8,128)(2,1)S(1)}, bf16[1024,256]{0,1:T(8,128)(2,1)S(1)}, u32[]{:S(2)}, u32[]{:S(2)}) collective-permute-start(bf16[1024,256]{0,1:T(8,128)(2,1)S(1)} %bitcast.84), channel_id=1, source_target_pairs={{0,704},{32,736},{64,0},{96,32},{128,64},{160,96},{192,128},{224,1... | collective-permute-start | bytes 1572872 | tf_op jit(solution)/shard_map/ppermute | solution.py:15

commit v2 on v1

v2 whole, which is shorter than its diff:
```python
import jax
import jax.numpy as jnp
from jax import lax
from jax.experimental import pallas as pl
from jax.experimental.pallas import tpu as pltpu
from jax.sharding import PartitionSpec as P

MESH = pl.DeviceIdType.MESH
NR = 24
NC = 32
W = 128
M = 8
LT = 3
RT = 4
ROWS = 512
CHUNKS = 4
DEEP = M * W // CHUNKS


def spread(c):
    return c // 8, (c // 2) % 4, c % 2


def joined(x, y, k):
    return lax.rem(x + 4, 4) * 8 + lax.rem(y + 4, 4) * 2 + lax.rem(k + 2, 2)


def kernel(
    meta, pattern, density, blocks, out,
    blk, a_own, a_ext, a_r1, a_r2, send, recv, relay, msend, mrecv, mrelay,
    acc, acc_x, b_own, b_ext, b_r1, b_r2,
    in_sem, d_send, d_recv, m_send, m_recv, y_send, y_recv, n_send, n_recv,
    a2_send, a2_recv, a1_send, a1_recv, b2_send, b2_recv, b1_send, b1_recv,
):
    r = lax.axis_index("row")
    c = lax.axis_index("col")
    x, y, k = spread(c)

    def at_offset(d, sign):
        dx, dy, dk = spread(d)
        return joined(x + sign * dx, y + sign * dy, k + dk)

    barrier = pltpu.get_barrier_semaphore()

    def greet(d, carry):
        pl.semaphore_signal(
            barrier, inc=1, device_id=(r, lax.rem(c + d, NC)), device_id_type=MESH
        )
        return carry

    lax.fori_loop(1, NC, greet, 0)
    near = r + 1 - 2 * lax.rem(r, 2)
    above = lax.rem(r + 2, NR)
    below = lax.rem(r + NR - 2, NR)
    pl.semaphore_signal(barrier, inc=1, device_id=(near, c), device_id_type=MESH)
    pl.semaphore_signal(barrier, inc=1, device_id=(above, c), device_id_type=MESH)

    own_first = (r + c) // NC
    ext_first = (r + lax.rem(c + NC - 2, NC) + 2) // NC

    def block_load():
        return pltpu.make_async_copy(blocks, blk, in_sem.at[0])

    def panel_load(first, place, sem, m):
        return pltpu.make_async_copy(
            density.at[:, pl.ds(pl.multiple_of((first + LT * m) * W, W), W)],
            place.at[:, m * W:(m + 1) * W],
            in_sem.at[sem + m],
        )

    block_load().start()
    for m in range(M):
        panel_load(ext_first, a_ext, 1, m).start()
    for m in range(M):
        panel_load(own_first, a_own, 1 + M, m).start()

    block_load().wait()

    def pack(d, carry):
        owner = at_offset(d, 1)
        low = meta[0, owner]
        high = meta[1, owner]
        send[d, 0] = blk[jnp.maximum(low, 0) // 64]
        send[d, 1] = blk[jnp.maximum(high, 0) // 64]
        low = jnp.where(low < 0, -1, lax.rem(jnp.maximum(low, 0), 64))
        high = jnp.where(high < 0, -1, lax.rem(jnp.maximum(high, 0), 64))
        msend[d, 0:1] = jnp.full((1, W), low, jnp.int32)
        msend[d, 1:2] = jnp.full((1, W), high, jnp.int32)
        return carry

    lax.fori_loop(0, NC, pack, 0)

    def gate(first, place):
        def one(i, carry):
            rows = pl.ds(pl.multiple_of(i * W, W), W)
            for m in range(M):
                keep = pattern[i, first + LT * m] != 0
                value = place[rows, m * W:(m + 1) * W]
                place[rows, m * W:(m + 1) * W] = jnp.where(keep, value, jnp.zeros_like(value))
            return carry

        lax.fori_loop(0, ROWS // W, one, 0)

    for m in range(M):
        panel_load(ext_first, a_ext, 1, m).wait()
    gate(ext_first, a_ext)

    pl.semaphore_wait(barrier, NC + 1)

    def direct(d):
        to = (r, at_offset(d, 1))
        return (
            pltpu.make_async_remote_copy(
                send.at[d], recv.at[d], d_send.at[d], d_recv.at[d], device_id=to, device_id_type=MESH
            ),
            pltpu.make_async_remote_copy(
                msend.at[d], mrecv.at[d], m_send.at[d], m_recv.at[d], device_id=to, device_id_type=MESH
            ),
        )

    def offset_of(e, dy):
        return (e // 2) * 8 + dy * 2 + lax.rem(e, 2)

    def first_leg(e):
        d = offset_of(e, 2)
        to = (r, at_offset(offset_of(e, 1), 1))
        return (
            pltpu.make_async_remote_copy(
                send.at[d], relay.at[e], d_send.at[d], y_recv.at[e], device_id=to, device_id_type=MESH
            ),
            pltpu.make_async_remote_copy(
                msend.at[d], mrelay.at[e], m_send.at[d], n_recv.at[e], device_id=to, device_id_type=MESH
            ),
        )

    def second_leg(e):
        d = offset_of(e, 2)
        to = (r, joined(x, y + 1, k))
        return (
            pltpu.make_async_remote_copy(
                relay.at[e], recv.at[d], y_send.at[e], d_recv.at[d], device_id=to, device_id_type=MESH
            ),
            pltpu.make_async_remote_copy(
                mrelay.at[e], mrecv.at[d], n_send.at[e], m_recv.at[d], device_id=to, device_id_type=MESH
            ),
        )

    def panel_shift(i):
        rows = pl.ds(pl.multiple_of(i * W, W), W)
        return pltpu.make_async_remote_copy(
            a_ext.at[rows], a_r2.at[rows], a2_send.at[i], a2_recv.at[i],
            device_id=(r, lax.rem(c + NC - 2, NC)), device_id_type=MESH,
        )

    def panel_across(source, i):
        rows = pl.ds(pl.multiple_of(i * W, W), W)
        return pltpu.make_async_remote_copy(
            source.at[rows], a_r1.at[rows], a1_send.at[i], a1_recv.at[i],
            device_id=(r, c + 1 - 2 * k), device_id_type=MESH,
        )

    def go(pair):
        for one in pair:
            one.start()

    def send_out(e, carry):
        go(first_leg(e))
        go(direct(offset_of(e, 3)))
        go(direct(offset_of(e, 1)))

        @pl.when(e % 2 == 1)
        def _():
            panel_shift(e // 2).start()

        @pl.when(e > 0)
        def _():
            go(direct(offset_of(e, 0)))

        return carry

    lax.fori_loop(0, 8, send_out, 0)

    recv[0] = send[0]
    mrecv[0] = msend[0]
    for m in range(M):
        panel_load(own_first, a_own, 1 + M, m).wait()
    gate(own_first, a_own)

    @pl.when(k == 1)
    def _():
        def one(i, carry):
            panel_across(a_own, i).start()
            return carry

        lax.fori_loop(0, CHUNKS, one, 0)

    def pass_on(e, carry):
        for one in first_leg(e):
            one.wait_recv()
        go(second_leg(e))
        return carry

    lax.fori_loop(0, 8, pass_on, 0)

    right_first = (r + c) // NR

    def gathered(position, first, dy):
        wanted = 2 * first + 8 * (position // 2) + lax.rem(position, 2)
        total = jnp.zeros((W, W), jnp.float32)
        for e in range(8):
            d = (e // 2) * 8 + dy * 2 + e % 2
            for s in range(2):
                hit = jnp.broadcast_to(mrecv[d, s:s + 1], (W, W)) == wanted
                total = total + jnp.where(hit, recv[d, s].astype(jnp.float32), 0.0)
        return total

    def where_at(m):
        return pl.ds(pl.multiple_of(m * W, W), W)

    def add_group(dy, fresh):
        def one(m, carry):
            for q in range(2):
                lanes = slice(q * W, (q + 1) * W)
                value = gathered(2 * m + q, right_first, dy)
                acc[where_at(m), lanes] = value if fresh else acc[where_at(m), lanes] + value

                @pl.when(r < 2)
                def _():
                    value = gathered(2 * m + q, right_first + 1, dy)
                    acc_x[where_at(m), lanes] = value if fresh else acc_x[where_at(m), lanes] + value

            return carry

        lax.fori_loop(0, M, one, 0)

    def arrived(dy):
        def one(e, carry):
            d = offset_of(e, dy)

            @pl.when(d > 0)
            def _():
                for copy in direct(d):
                    copy.wait_recv()

            return carry

        lax.fori_loop(0, 8, one, 0)

    arrived(0)
    add_group(0, True)
    arrived(3)
    add_group(3, False)
    arrived(1)
    add_group(1, False)
    arrived(2)

    def down_two(ch):
        rows = pl.ds(pl.multiple_of(ch * DEEP, DEEP), DEEP)
        return pltpu.make_async_remote_copy(
            b_ext.at[rows], b_r2.at[rows], b2_send.at[ch], b2_recv.at[ch],
            device_id=(below, c), device_id_type=MESH,
        )

    def beside(source, ch):
        rows = pl.ds(pl.multiple_of(ch * DEEP, DEEP), DEEP)
        return pltpu.make_async_remote_copy(
            source.at[rows], b_r1.at[rows], b1_send.at[ch], b1_recv.at[ch],
            device_id=(near, c), device_id_type=MESH,
        )

    odd = lax.rem(r, 2) == 1

    def finish(ch, carry):
        for half in range(M // CHUNKS):
            m = ch * (M // CHUNKS) + half
            for q in range(2):
                lanes = slice(q * W, (q + 1) * W)
                value = (acc[where_at(m), lanes] + gathered(2 * m + q, right_first, 2)).astype(jnp.bfloat16)
                b_own[where_at(m), lanes] = value

                @pl.when(r >= 2)
                def _():
                    b_ext[where_at(m), lanes] = value

                @pl.when(r < 2)
                def _():
                    b_ext[where_at(m), lanes] = (
                        acc_x[where_at(m), lanes] + gathered(2 * m + q, right_first + 1, 2)
                    ).astype(jnp.bfloat16)

        down_two(ch).start()

        @pl.when(odd)
        def _():
            beside(b_own, ch).start()

        return carry

    lax.fori_loop(0, CHUNKS, finish, 0)

    def add_product(left, right, ch):
        depth = pl.ds(pl.multiple_of(ch * DEEP, DEEP), DEEP)
        out[...] += jnp.dot(left[:, depth], right[depth, :], preferred_element_type=jnp.float32)

    def panel_arrives(i, carry):
        panel_shift(i).wait_recv()

        @pl.when(k == 0)
        def _():
            panel_across(a_r2, i).start()

        return carry

    lax.fori_loop(0, CHUNKS, panel_arrives, 0)
    out[...] = jnp.zeros_like(out)

    def local_part(ch, carry):
        add_product(a_own, b_own, ch)
        return carry

    lax.fori_loop(0, CHUNKS, local_part, 0)

    def two_up(ch, carry):
        down_two(ch).wait_recv()

        @pl.when(jnp.logical_not(odd))
        def _():
            beside(b_r2, ch).start()

        add_product(a_r2, b_r2, ch)
        return carry

    lax.fori_loop(0, CHUNKS, two_up, 0)

    def across_arrives(i, carry):
        panel_across(a_own, i).wait_recv()
        return carry

    lax.fori_loop(0, CHUNKS, across_arrives, 0)

    def one_up(ch, carry):
        beside(b_own, ch).wait_recv()
        add_product(a_r1, b_r1, ch)
        return carry

    lax.fori_loop(0, CHUNKS, one_up, 0)

    def sent(d, carry):
        for copy in direct(d):
            copy.wait_send()
        return carry

    lax.fori_loop(1, NC, sent, 0)

    def passed(e, carry):
        for copy in second_leg(e):
            copy.wait_send()
        return carry

    lax.fori_loop(0, 8, passed, 0)

    def rest(i, carry):
        panel_shift(i).wait_send()
        panel_across(a_own, i).wait_send()
        down_two(i).wait_send()
        beside(b_own, i).wait_send()
        return carry

    lax.fori_loop(0, CHUNKS, rest, 0)


def on_device(density_panel, density_pattern, margin_blocks, margin_owner, margin_place):
    stack = margin_blocks.shape[1]
    owners = margin_owner[0, :, 0]
    code = jnp.arange(stack) * 64 + margin_place[0]
    mine = owners[None, :] == jnp.arange(NC)[:, None]
    low = jnp.min(jnp.where(mine, code[None, :], stack * 64), axis=1)
    high = jnp.max(jnp.where(mine, code[None, :], -1), axis=1)
    meta = jnp.stack([jnp.where(high < 0, -1, low), jnp.where(high == low, -1, high)])
    bf16, f32, i32 = jnp.bfloat16, jnp.float32, jnp.int32
    dma = pltpu.SemaphoreType.DMA
    return pl.pallas_call(
        kernel,
        out_shape=jax.ShapeDtypeStruct((ROWS, 2 * W), f32),
        in_specs=[
            pl.BlockSpec(memory_space=pltpu.SMEM),
            pl.BlockSpec(memory_space=pltpu.SMEM),
            pl.BlockSpec(memory_space=pl.ANY),
            pl.BlockSpec(memory_space=pl.ANY),
        ],
        out_specs=pl.BlockSpec(memory_space=pltpu.VMEM),
        scratch_shapes=[
            pltpu.VMEM((stack, W, W), bf16),
            pltpu.VMEM((ROWS, M * W), bf16),
            pltpu.VMEM((ROWS, M * W), bf16),
            pltpu.VMEM((ROWS, M * W), bf16),
            pltpu.VMEM((ROWS, M * W), bf16),
            pltpu.VMEM((NC, 2, W, W), bf16),
            pltpu.VMEM((NC, 2, W, W), bf16),
            pltpu.VMEM((8, 2, W, W), bf16),
            pltpu.VMEM((NC, 2, W), i32),
            pltpu.VMEM((NC, 2, W), i32),
            pltpu.VMEM((8, 2, W), i32),
            pltpu.VMEM((M * W, 2 * W), f32),
            pltpu.VMEM((M * W, 2 * W), f32),
            pltpu.VMEM((M * W, 2 * W), bf16),
            pltpu.VMEM((M * W, 2 * W), bf16),
            pltpu.VMEM((M * W, 2 * W), bf16),
            pltpu.VMEM((M * W, 2 * W), bf16),
            dma((1 + 2 * M,)),
            dma((NC,)), dma((NC,)), dma((NC,)), dma((NC,)),
            dma((8,)), dma((8,)), dma((8,)), dma((8,)),
            dma((CHUNKS,)), dma((CHUNKS,)), dma((CHUNKS,)), dma((CHUNKS,)),
            dma((CHUNKS,)), dma((CHUNKS,)), dma((CHUNKS,)), dma((CHUNKS,)),
        ],
        compiler_params=pltpu.CompilerParams(
            collective_id=0, has_side_effects=True, vmem_limit_bytes=48 * 1024 * 1024
        ),
        cost_estimate=pl.CostEstimate(flops=2 * ROWS * 3 * M * W * 2 * W, bytes_accessed=6 << 20, transcendentals=0),
    )(meta, density_pattern, density_panel, margin_blocks[0])


def solution(mesh):
    return jax.shard_map(
        on_device,
        mesh=mesh,
        in_specs=(
            P("row", "col"),
            P("row", "col"),
            P("row", "col", None, None),
            P("row", "col", None),
            P("row", "col"),
        ),
        out_specs=P("row", "col"),
        check_vma=False,
    )
```

time: 161 us -> 115 us (0.71)
  the two profiles are of different devices: /device:TPU:6 before, /device:TPU:27 now
where the time goes in v2:
time: 115 us
  Pallas kernels  109 us (95%)
  local copies, waits for them, and re-layouts  4.59 us (4%)
  other arithmetic  1.45 us (1%)
    pallas_call x1, Pallas kernels, on_device(): pl.pallas_call(kernel, out_shape=jax.ShapeDtypeStruct((ROWS, 2 * W), f32)...  109 us
    unnamed x7, local copies, waits for them, and re-layouts  4.59 us

profile of v2, /device:TPU:27, one launch (start us, length us, event | category | flops | bytes accessed | tf_op | source)
XLA Modules:
  0.0 115.1 jit_solution(5551088290236336630)
XLA Ops:
  0.0 0.7 add_bitcast_fusion
  0.7 0.8 select_reduce_fusion.1
  1.5 0.0 copy-start
  1.5 1.9 %copy-done = bf16[512,3072]{1,0:T(8,128)(2,1)S(1)} copy-done((bf16[512,3072]{1,0:T(8,128)(2,1)S(1)}, bf16[512,3072]{1,0:T(8,128)(2,1)}, u32[]{:S(2)}) %copy-start) | copy-done | bytes 3145752
  3.4 0.0 copy-start.1
  3.4 1.2 %copy-done.1 = bf16[1,32,128,128]{3,2,1,0:T(8,128)(2,1)S(1)} copy-done((bf16[1,32,128,128]{3,2,1,0:T(8,128)(2,1)S(1)}, bf16[1,32,128,128]{3,2,1,0:T(8,128)(2,1)}, u32[]{:S(2)}) %copy-start.1) | copy-done | bytes 1048600
  4.6 0.0 copy-start.2
  4.6 0.7 copy-done.2
  5.3 109.0 %shard_map.55 = f32[512,256]{1,0:T(8,128)S(1)} custom-call(s32[2,32]{1,0:T(2,128)S(1)} %pad_add_fusion.meta, s32[4,24]{1,0:T(4,128)S(1)} %copy-done.2, bf16[512,3072]{1,0:T(8,128)(2,1)S(1)} %copy-done, bf16[32,128,128]{2,1,0:T(8,128)(2,1)S(1)} %bitcast.10), custom_call_target="tpu_custom_call" | custom-call | flops 805306368 | bytes 6291456 | tf_op jit(solution)/shard_map/pallas_call | solution.py:382
  114.3 0.8 copy.7
  (2 shorter events, 0.0 us)
Async XLA Ops:
  1.5 1.9 %copy-start = (bf16[512,3072]{1,0:T(8,128)(2,1)S(1)}, bf16[512,3072]{1,0:T(8,128)(2,1)}, u32[]{:S(2)}) copy-start(bf16[512,3072]{1,0:T(8,128)(2,1)} %density.1) | copy-start | bytes 9437188
  3.4 1.2 %copy-start.1 = (bf16[1,32,128,128]{3,2,1,0:T(8,128)(2,1)S(1)}, bf16[1,32,128,128]{3,2,1,0:T(8,128)(2,1)}, u32[]{:S(2)}) copy-start(bf16[1,32,128,128]{3,2,1,0:T(8,128)(2,1)} %param.7) | copy-start | bytes 3145732
  4.6 0.7 copy-start.2

commit v3 on v2

--- a/solution.py
+++ b/solution.py
@@ -26,7 +26,7 @@
 
 
 def kernel(
-    meta, pattern, density, blocks, out,
+    low, high, places, pattern, density, blocks, out,
     blk, a_own, a_ext, a_r1, a_r2, send, recv, relay, msend, mrecv, mrelay,
     acc, acc_x, b_own, b_ext, b_r1, b_r2,
     in_sem, d_send, d_recv, m_send, m_recv, y_send, y_recv, n_send, n_recv,
@@ -74,21 +74,18 @@
     for m in range(M):
         panel_load(own_first, a_own, 1 + M, m).start()
 
-    block_load().wait()
-
-    def pack(d, carry):
+    def pack(d):
         owner = at_offset(d, 1)
-        low = meta[0, owner]
-        high = meta[1, owner]
-        send[d, 0] = blk[jnp.maximum(low, 0) // 64]
-        send[d, 1] = blk[jnp.maximum(high, 0) // 64]
-        low = jnp.where(low < 0, -1, lax.rem(jnp.maximum(low, 0), 64))
-        high = jnp.where(high < 0, -1, lax.rem(jnp.maximum(high, 0), 64))
-        msend[d, 0:1] = jnp.full((1, W), low, jnp.int32)
-        msend[d, 1:2] = jnp.full((1, W), high, jnp.int32)
-        return carry
-
-    lax.fori_loop(0, NC, pack, 0)
+        one = low[owner]
+        two = high[owner]
+        first = jnp.where(two < 0, 0, one)
+        second = jnp.maximum(two, 0)
+        send[d, 0] = blk[first]
+        send[d, 1] = blk[second]
+        first = jnp.where(two < 0, -1, places[0, first])
+        second = jnp.where((two < 0) | (two == one), -1, places[0, second])
+        msend[d, 0:1] = jnp.full((1, W), first, jnp.int32)
+        msend[d, 1:2] = jnp.full((1, W), second, jnp.int32)
 
     def gate(first, place):
         def one(i, carry):
@@ -101,10 +98,7 @@
 
         lax.fori_loop(0, ROWS // W, one, 0)
 
-    for m in range(M):
-        panel_load(ext_first, a_ext, 1, m).wait()
-    gate(ext_first, a_ext)
-
+    block_load().wait()
     pl.semaphore_wait(barrier, NC + 1)
 
     def direct(d):
@@ -163,14 +157,20 @@
         for one in pair:
             one.start()
 
-    def send_out(e, carry):
+    def send_first(e, carry):
+        pack(offset_of(e, 2))
         go(first_leg(e))
+        pack(offset_of(e, 3))
         go(direct(offset_of(e, 3)))
+        return carry
+
+    lax.fori_loop(0, 8, send_first, 0)
+
+    def send_next(e, carry):
+        pack(offset_of(e, 1))
         go(direct(offset_of(e, 1)))
 
-        @pl.when(e % 2 == 1)
-        def _():
-            panel_shift(e // 2).start()
+        pack(offset_of(e, 0))
 
         @pl.when(e > 0)
         def _():
@@ -178,7 +178,17 @@
 
         return carry
 
-    lax.fori_loop(0, 8, send_out, 0)
+    lax.fori_loop(0, 8, send_next, 0)
+
+    for m in range(M):
+        panel_load(ext_first, a_ext, 1, m).wait()
+    gate(ext_first, a_ext)
+
+    def send_panel(i, carry):
+        panel_shift(i).start()
+        return carry
+
+    lax.fori_loop(0, CHUNKS, send_panel, 0)
 
     recv[0] = send[0]
     mrecv[0] = msend[0]
@@ -204,55 +214,66 @@
 
     right_first = (r + c) // NR
 
-    def gathered(position, first, dy):
-        wanted = 2 * first + 8 * (position // 2) + lax.rem(position, 2)
-        total = jnp.zeros((W, W), jnp.float32)
-        for e in range(8):
-            d = (e // 2) * 8 + dy * 2 + e % 2
-            for s in range(2):
-                hit = jnp.broadcast_to(mrecv[d, s:s + 1], (W, W)) == wanted
-                total = total + jnp.where(hit, recv[d, s].astype(jnp.float32), 0.0)
-        return total
-
     def where_at(m):
         return pl.ds(pl.multiple_of(m * W, W), W)
 
-    def add_group(dy, fresh):
-        def one(m, carry):
-            for q in range(2):
-                lanes = slice(q * W, (q + 1) * W)
-                value = gathered(2 * m + q, right_first, dy)
-                acc[where_at(m), lanes] = value if fresh else acc[where_at(m), lanes] + value
-
-                @pl.when(r < 2)
-                def _():
-                    value = gathered(2 * m + q, right_first + 1, dy)
-                    acc_x[where_at(m), lanes] = value if fresh else acc_x[where_at(m), lanes] + value
-
-            return carry
-
-        lax.fori_loop(0, M, one, 0)
-
-    def arrived(dy):
-        def one(e, carry):
-            d = offset_of(e, dy)
-
-            @pl.when(d > 0)
-            def _():
-                for copy in direct(d):
-                    copy.wait_recv()
-
-            return carry
-
-        lax.fori_loop(0, 8, one, 0)
-
-    arrived(0)
-    add_group(0, True)
-    arrived(3)
-    add_group(3, False)
-    arrived(1)
-    add_group(1, False)
-    arrived(2)
+    def add_pair(d):
+        values = [recv[d, s].astype(jnp.float32).reshape(W // 8, 8, W) for s in range(2)]
+        places = [jnp.broadcast_to(mrecv[d, s:s + 1], (8, W)) for s in range(2)]
+
+        def into(sums, first):
+            def one(m, carry):
+                for q in range(2):
+                    total = sums[2 * m + q]
+                    for s in range(2):
+                        hit = (places[s] == 2 * first + 8 * m + q)[None]
+                        total = total + jnp.where(hit, values[s], 0.0)
+                    sums[2 * m + q] = total
+                return carry
+
+            lax.fori_loop(0, M, one, 0)
+
+        into(acc, right_first)
+
+        @pl.when(r < 2)
+        def _():
+            into(acc_x, right_first + 1)
+
+    def take(d):
+        for copy in direct(d):
+            copy.wait_recv()
+        add_pair(d)
+
+    def clear(position, carry):
+        acc[position] = jnp.zeros((W // 8, 8, W), jnp.float32)
+        acc_x[position] = jnp.zeros((W // 8, 8, W), jnp.float32)
+        return carry
+
+    lax.fori_loop(0, 2 * M, clear, 0)
+    add_pair(0)
+
+    def take_behind(e, carry):
+        take(offset_of(e, 3))
+        return carry
+
+    lax.fori_loop(0, 8, take_behind, 0)
+
+    def take_ahead(e, carry):
+        take(offset_of(e, 1))
+
+        @pl.when(e > 0)
+        def _():
+            take(offset_of(e, 0))
+
+        return carry
+
+    lax.fori_loop(0, 8, take_ahead, 0)
+
+    def take_far(e, carry):
+        take(offset_of(e, 2))
+        return carry
+
+    lax.fori_loop(0, 8, take_far, 0)
 
     def down_two(ch):
         rows = pl.ds(pl.multiple_of(ch * DEEP, DEEP), DEEP)
@@ -275,7 +296,7 @@
             m = ch * (M // CHUNKS) + half
             for q in range(2):
                 lanes = slice(q * W, (q + 1) * W)
-                value = (acc[where_at(m), lanes] + gathered(2 * m + q, right_first, 2)).astype(jnp.bfloat16)
+                value = acc[2 * m + q].reshape(W, W).astype(jnp.bfloat16)
                 b_own[where_at(m), lanes] = value
 
                 @pl.when(r >= 2)
@@ -284,9 +305,7 @@
 
                 @pl.when(r < 2)
                 def _():
-                    b_ext[where_at(m), lanes] = (
-                        acc_x[where_at(m), lanes] + gathered(2 * m + q, right_first + 1, 2)
-                    ).astype(jnp.bfloat16)
+                    b_ext[where_at(m), lanes] = acc_x[2 * m + q].reshape(W, W).astype(jnp.bfloat16)
 
         down_two(ch).start()
 
@@ -372,17 +391,18 @@
 def on_device(density_panel, density_pattern, margin_blocks, margin_owner, margin_place):
     stack = margin_blocks.shape[1]
     owners = margin_owner[0, :, 0]
-    code = jnp.arange(stack) * 64 + margin_place[0]
+    index = jnp.arange(stack)[None, :]
     mine = owners[None, :] == jnp.arange(NC)[:, None]
-    low = jnp.min(jnp.where(mine, code[None, :], stack * 64), axis=1)
-    high = jnp.max(jnp.where(mine, code[None, :], -1), axis=1)
-    meta = jnp.stack([jnp.where(high < 0, -1, low), jnp.where(high == low, -1, high)])
+    high = jnp.max(jnp.where(mine, index, -1), axis=1)
+    low = jnp.min(jnp.where(mine, index, stack), axis=1)
     bf16, f32, i32 = jnp.bfloat16, jnp.float32, jnp.int32
     dma = pltpu.SemaphoreType.DMA
     return pl.pallas_call(
         kernel,
         out_shape=jax.ShapeDtypeStruct((ROWS, 2 * W), f32),
         in_specs=[
+            pl.BlockSpec(memory_space=pltpu.SMEM),
+            pl.BlockSpec(memory_space=pltpu.SMEM),
             pl.BlockSpec(memory_space=pltpu.SMEM),
             pl.BlockSpec(memory_space=pltpu.SMEM),
             pl.BlockSpec(memory_space=pl.ANY),
@@ -401,8 +421,8 @@
             pltpu.VMEM((NC, 2, W), i32),
             pltpu.VMEM((NC, 2, W), i32),
             pltpu.VMEM((8, 2, W), i32),
-            pltpu.VMEM((M * W, 2 * W), f32),
-            pltpu.VMEM((M * W, 2 * W), f32),
+            pltpu.VMEM((2 * M, W // 8, 8, W), f32),
+            pltpu.VMEM((2 * M, W // 8, 8, W), f32),
             pltpu.VMEM((M * W, 2 * W), bf16),
             pltpu.VMEM((M * W, 2 * W), bf16),
             pltpu.VMEM((M * W, 2 * W), bf16),
@@ -414,10 +434,10 @@
             dma((CHUNKS,)), dma((CHUNKS,)), dma((CHUNKS,)), dma((CHUNKS,)),
         ],
         compiler_params=pltpu.CompilerParams(
-            collective_id=0, has_side_effects=True, vmem_limit_bytes=48 * 1024 * 1024
+            collective_id=0, has_side_effects=True, vmem_limit_bytes=62 * 1024 * 1024
         ),
         cost_estimate=pl.CostEstimate(flops=2 * ROWS * 3 * M * W * 2 * W, bytes_accessed=6 << 20, transcendentals=0),
-    )(meta, density_pattern, density_panel, margin_blocks[0])
+    )(low, high, margin_place, density_pattern, density_panel, margin_blocks[0])
 
 
 def solution(mesh):

time: 115 us -> 107 us (0.930)
  the two profiles are of different devices: /device:TPU:27 before, /device:TPU:6 now
where the time goes in v3:
time: 107 us
  Pallas kernels  103 us (96%)
  local copies, waits for them, and re-layouts  1.87 us (2%)
  other arithmetic  1.37 us (1%)
    pallas_call x1, Pallas kernels, on_device(): pl.pallas_call(kernel, out_shape=jax.ShapeDtypeStruct((ROWS, 2 * W), f32)...  103 us

profile of v3, /device:TPU:6, one launch (start us, length us, event | category | flops | bytes accessed | tf_op | source)
XLA Modules:
  0.0 106.6 jit_solution(10013855247835093967)
XLA Ops:
  0.0 1.4 %select_reduce_fusion = (s32[32]{0:T(128)}, s32[32]{0:T(128)}) fusion(s32[32]{0:T(128)} %bitcast.3), kind=kLoop, calls=%fused_computation | loop fusion | flops 5056 | bytes 384 | tf_op jit(solution)/shard_map/reduce_max | solution.py:396
  1.4 103.4 %shard_map.55 = f32[512,256]{1,0:T(8,128)} custom-call(s32[32]{0:T(128)} %get-tuple-element.6.low, s32[32]{0:T(128)} %get-tuple-element.5.high, s32[1,32]{1,0:T(1,128)} %places.1, s32[4,24]{1,0:T(4,128)} %pattern.1, bf16[512,3072]{1,0:T(8,128)(2,1)} %density.1, bf16[32,128,128]{2,1,0:T(8,128)(2,1)} %bitcast.2), custom_call_target="tpu_custom_call" | custom-call | flops 805306368 | bytes 6291456 | tf_op jit(solution)/shard_map/pallas_call | solution.py:400
  104.8 1.9 %copy.7 = f32[512,256]{1,0:T(8,128)} copy(f32[512,256]{1,0:T(8,128)} %shard_map.55) | data formatting | bytes 1048576

commit v4 on v3

v4 whole, which is shorter than its diff:
```python
import functools

import jax
import jax.numpy as jnp
from jax import lax
from jax.experimental import pallas as pl
from jax.experimental.pallas import tpu as pltpu
from jax.sharding import PartitionSpec as P

MESH = pl.DeviceIdType.MESH
NR = 24
NC = 32
W = 128
M = 8
LT = 3
RT = 4
ROWS = 512
CHUNKS = 4
DEEP = M * W // CHUNKS
H = W // 2


def spread(c):
    return c // 8, (c // 2) % 4, c % 2


def joined(x, y, k):
    return lax.rem(x + 4, 4) * 8 + lax.rem(y + 4, 4) * 2 + lax.rem(k + 2, 2)


def kernel(
    low, high, places, pattern, density, blocks, out,
    blk, a_own, a_ext, a_r1, a_r2, send, recv, relay, msend, mrecv, mrelay,
    acc, acc_x, b_own, b_ext, b_r1, b_r2,
    in_sem, d_send, d_recv, m_send, m_recv, y_send, y_recv, n_send, n_recv,
    a2_send, a2_recv, a1_send, a1_recv, b2_send, b2_recv, b1_send, b1_recv,
):
    r = lax.axis_index("row")
    c = lax.axis_index("col")
    x, y, k = spread(c)

    def at_offset(d, sign):
        dx, dy, dk = spread(d)
        return joined(x + sign * dx, y + sign * dy, k + dk)

    barrier = pltpu.get_barrier_semaphore()

    def greet(d, carry):
        pl.semaphore_signal(
            barrier, inc=1, device_id=(r, lax.rem(c + d, NC)), device_id_type=MESH
        )
        return carry

    lax.fori_loop(1, NC, greet, 0)
    near = r + 1 - 2 * lax.rem(r, 2)
    above = lax.rem(r + 2, NR)
    below = lax.rem(r + NR - 2, NR)
    pl.semaphore_signal(barrier, inc=1, device_id=(near, c), device_id_type=MESH)
    pl.semaphore_signal(barrier, inc=1, device_id=(above, c), device_id_type=MESH)

    own_first = (r + c) // NC
    ext_first = (r + lax.rem(c + NC - 2, NC) + 2) // NC

    def block_load():
        return pltpu.make_async_copy(blocks, blk, in_sem.at[0])

    def panel_load(first, place, sem, m):
        return pltpu.make_async_copy(
            density.at[:, pl.ds(pl.multiple_of((first + LT * m) * W, W), W)],
            place.at[:, m * W:(m + 1) * W],
            in_sem.at[sem + m],
        )

    block_load().start()
    for m in range(M):
        panel_load(ext_first, a_ext, 1, m).start()
    for m in range(M):
        panel_load(own_first, a_own, 1 + M, m).start()

    def pack(d):
        owner = at_offset(d, 1)
        one = low[owner]
        two = high[owner]
        first = jnp.where(two < 0, 0, one)
        second = jnp.maximum(two, 0)
        for slot, value in ((0, blk[first]), (1, blk[second])):
            send[d, 0, slot] = value[:H]
            send[d, 1, slot] = value[H:]
        first = jnp.where(two < 0, -1, places[0, first])
        second = jnp.where((two < 0) | (two == one), -1, places[0, second])
        msend[d, 0:1] = jnp.full((1, W), first, jnp.int32)
        msend[d, 1:2] = jnp.full((1, W), second, jnp.int32)

    def gate(first, place):
        def one(i, carry):
            rows = pl.ds(pl.multiple_of(i * W, W), W)
            for m in range(M):
                keep = pattern[i, first + LT * m] != 0
                value = place[rows, m * W:(m + 1) * W]
                place[rows, m * W:(m + 1) * W] = jnp.where(keep, value, jnp.zeros_like(value))
            return carry

        lax.fori_loop(0, ROWS // W, one, 0)

    block_load().wait()
    pl.semaphore_wait(barrier, NC + 1)

    def direct(d, h):
        return pltpu.make_async_remote_copy(
            send.at[d, h], recv.at[d, h], d_send.at[d, h], d_recv.at[d, h],
            device_id=(r, at_offset(d, 1)), device_id_type=MESH,
        )

    def direct_place(d):
        return pltpu.make_async_remote_copy(
            msend.at[d], mrecv.at[d], m_send.at[d], m_recv.at[d],
            device_id=(r, at_offset(d, 1)), device_id_type=MESH,
        )

    def offset_of(e, dy):
        return (e // 2) * 8 + dy * 2 + lax.rem(e, 2)

    def first_leg(e, h):
        d = offset_of(e, 2)
        return pltpu.make_async_remote_copy(
            send.at[d, h], relay.at[e, h], d_send.at[d, h], y_recv.at[e, h],
            device_id=(r, at_offset(offset_of(e, 1), 1)), device_id_type=MESH,
        )

    def first_place(e):
        d = offset_of(e, 2)
        return pltpu.make_async_remote_copy(
            msend.at[d], mrelay.at[e], m_send.at[d], n_recv.at[e],
            device_id=(r, at_offset(offset_of(e, 1), 1)), device_id_type=MESH,
        )

    def second_leg(e, h):
        d = offset_of(e, 2)
        return pltpu.make_async_remote_copy(
            relay.at[e, h], recv.at[d, h], y_send.at[e, h], d_recv.at[d, h],
            device_id=(r, joined(x, y + 1, k)), device_id_type=MESH,
        )

    def second_place(e):
        d = offset_of(e, 2)
        return pltpu.make_async_remote_copy(
            mrelay.at[e], mrecv.at[d], n_send.at[e], m_recv.at[d],
            device_id=(r, joined(x, y + 1, k)), device_id_type=MESH,
        )

    def panel_shift(i):
        rows = pl.ds(pl.multiple_of(i * W, W), W)
        return pltpu.make_async_remote_copy(
            a_ext.at[rows], a_r2.at[rows], a2_send.at[i], a2_recv.at[i],
            device_id=(r, lax.rem(c + NC - 2, NC)), device_id_type=MESH,
        )

    def panel_across(source, i):
        rows = pl.ds(pl.multiple_of(i * W, W), W)
        return pltpu.make_async_remote_copy(
            source.at[rows], a_r1.at[rows], a1_send.at[i], a1_recv.at[i],
            device_id=(r, c + 1 - 2 * k), device_id_type=MESH,
        )

    def send_first(e, carry):
        pack(offset_of(e, 2))
        first_place(e).start()
        first_leg(e, 0).start()
        pack(offset_of(e, 3))
        direct_place(offset_of(e, 3)).start()
        direct(offset_of(e, 3), 0).start()
        return carry

    lax.fori_loop(0, 8, send_first, 0)

    def send_next(e, carry):
        pack(offset_of(e, 1))
        direct_place(offset_of(e, 1)).start()
        direct(offset_of(e, 1), 0).start()
        pack(offset_of(e, 0))

        @pl.when(e > 0)
        def _():
            direct_place(offset_of(e, 0)).start()
            direct(offset_of(e, 0), 0).start()

        return carry

    lax.fori_loop(0, 8, send_next, 0)

    def send_second(e, carry):
        first_leg(e, 1).start()
        direct(offset_of(e, 3), 1).start()
        direct(offset_of(e, 1), 1).start()

        @pl.when(e > 0)
        def _():
            direct(offset_of(e, 0), 1).start()

        return carry

    lax.fori_loop(0, 8, send_second, 0)

    for m in range(M):
        panel_load(ext_first, a_ext, 1, m).wait()
    gate(ext_first, a_ext)

    recv[0] = send[0]
    mrecv[0] = msend[0]
    for m in range(M):
        panel_load(own_first, a_own, 1 + M, m).wait()
    gate(own_first, a_own)

    @pl.when(k == 1)
    def _():
        def one(i, carry):
            panel_across(a_own, i).start()
            return carry

        lax.fori_loop(0, CHUNKS, one, 0)

    def pass_on(e, carry):
        first_place(e).wait_recv()
        first_leg(e, 0).wait_recv()
        second_place(e).start()
        second_leg(e, 0).start()

        @pl.when(e % 2 == 1)
        def _():
            panel_shift(e // 2).start()

        return carry

    lax.fori_loop(0, 8, pass_on, 0)

    right_first = (r + c) // NR

    G = H // 8

    def add_pair(d, h):
        values = [recv[d, h, slot].astype(jnp.float32).reshape(G, 8, W) for slot in range(2)]
        places = [jnp.broadcast_to(mrecv[d, slot:slot + 1], (8, W)) for slot in range(2)]

        def into(sums, first):
            def one(m, carry):
                for q in range(2):
                    total = sums[2 * m + q, h * G:(h + 1) * G]
                    for slot in range(2):
                        hit = (places[slot] == 2 * first + 8 * m + q)[None]
                        total = total + jnp.where(hit, values[slot], 0.0)
                    sums[2 * m + q, h * G:(h + 1) * G] = total
                return carry

            lax.fori_loop(0, M, one, 0)

        into(acc, right_first)

        @pl.when(r < 2)
        def _():
            into(acc_x, right_first + 1)

    def take(d, h):
        if h == 0:
            direct_place(d).wait_recv()
        direct(d, h).wait_recv()
        add_pair(d, h)

    def clear(position, carry):
        acc[position] = jnp.zeros((W // 8, 8, W), jnp.float32)
        acc_x[position] = jnp.zeros((W // 8, 8, W), jnp.float32)
        return carry

    lax.fori_loop(0, 2 * M, clear, 0)
    odd = lax.rem(r, 2) == 1

    def down_two(ch, h):
        part = pl.ds(2 * ch, 2)
        return pltpu.make_async_remote_copy(
            b_ext.at[part, h], b_r2.at[part, h], b2_send.at[ch, h], b2_recv.at[ch, h],
            device_id=(below, c), device_id_type=MESH,
        )

    def beside(source, ch, h):
        part = pl.ds(2 * ch, 2)
        return pltpu.make_async_remote_copy(
            source.at[part, h], b_r1.at[part, h], b1_send.at[ch, h], b1_recv.at[ch, h],
            device_id=(near, c), device_id_type=MESH,
        )

    def finish(h):
        def one(ch, carry):
            for half in range(2):
                m = 2 * ch + half
                for q in range(2):
                    lanes = slice(q * W, (q + 1) * W)
                    value = acc[2 * m + q, h * G:(h + 1) * G].reshape(H, W).astype(jnp.bfloat16)
                    b_own[m, h, :, lanes] = value

                    @pl.when(r >= 2)
                    def _():
                        b_ext[m, h, :, lanes] = value

                    @pl.when(r < 2)
                    def _():
                        b_ext[m, h, :, lanes] = (
                            acc_x[2 * m + q, h * G:(h + 1) * G].reshape(H, W).astype(jnp.bfloat16)
                        )

            down_two(ch, h).start()

            @pl.when(odd)
            def _():
                beside(b_own, ch, h).start()

            return carry

        lax.fori_loop(0, CHUNKS, one, 0)

    def hand_on(ch, h):
        down_two(ch, h).wait_recv()

        @pl.when(jnp.logical_not(odd))
        def _():
            beside(b_r2, ch, h).start()

    def take_behind(e, carry, h):
        take(offset_of(e, 3), h)
        return carry

    def take_ahead(e, carry, h):
        if h == 0:
            first_leg(e, 1).wait_recv()
            second_leg(e, 1).start()
        take(offset_of(e, 1), h)

        @pl.when(e > 0)
        def _():
            take(offset_of(e, 0), h)

        return carry

    def take_far(e, carry, h):
        take(offset_of(e, 2), h)
        if h == 1:

            @pl.when(e % 2 == 1)
            def _():
                hand_on(e // 2, 0)

        return carry

    for h in range(2):
        add_pair(0, h)
        lax.fori_loop(0, 8, functools.partial(take_behind, h=h), 0)
        lax.fori_loop(0, 8, functools.partial(take_ahead, h=h), 0)
        lax.fori_loop(0, 8, functools.partial(take_far, h=h), 0)
        finish(h)

    def add_product(left, right, ch):
        depth = pl.ds(pl.multiple_of(ch * DEEP, DEEP), DEEP)
        piece = right[pl.ds(2 * ch, 2)].reshape(DEEP, 2 * W)
        out[...] += jnp.dot(left[:, depth], piece, preferred_element_type=jnp.float32)

    def panel_arrives(i, carry):
        panel_shift(i).wait_recv()

        @pl.when(k == 0)
        def _():
            panel_across(a_r2, i).start()

        return carry

    lax.fori_loop(0, CHUNKS, panel_arrives, 0)
    out[...] = jnp.zeros_like(out)

    def local_part(ch, carry):
        add_product(a_own, b_own, ch)
        return carry

    lax.fori_loop(0, CHUNKS, local_part, 0)

    def two_up(ch, carry):
        hand_on(ch, 1)
        add_product(a_r2, b_r2, ch)
        return carry

    lax.fori_loop(0, CHUNKS, two_up, 0)

    def across_arrives(i, carry):
        panel_across(a_own, i).wait_recv()
        return carry

    lax.fori_loop(0, CHUNKS, across_arrives, 0)

    def one_up(ch, carry):
        beside(b_own, ch, 0).wait_recv()
        beside(b_own, ch, 1).wait_recv()
        add_product(a_r1, b_r1, ch)
        return carry

    lax.fori_loop(0, CHUNKS, one_up, 0)

    def sent(d, carry):
        direct_place(d).wait_send()
        direct(d, 0).wait_send()
        direct(d, 1).wait_send()
        return carry

    lax.fori_loop(1, NC, sent, 0)

    def passed(e, carry):
        second_place(e).wait_send()
        second_leg(e, 0).wait_send()
        second_leg(e, 1).wait_send()
        return carry

    lax.fori_loop(0, 8, passed, 0)

    def rest(i, carry):
        panel_shift(i).wait_send()
        panel_across(a_own, i).wait_send()
        for h in range(2):
            down_two(i, h).wait_send()
            beside(b_own, i, h).wait_send()
        return carry

    lax.fori_loop(0, CHUNKS, rest, 0)


def on_device(density_panel, density_pattern, margin_blocks, margin_owner, margin_place):
    stack = margin_blocks.shape[1]
    owners = margin_owner[0, :, 0]
    index = jnp.arange(stack)[None, :]
    mine = owners[None, :] == jnp.arange(NC)[:, None]
    high = jnp.max(jnp.where(mine, index, -1), axis=1)
    low = jnp.min(jnp.where(mine, index, stack), axis=1)
    bf16, f32, i32 = jnp.bfloat16, jnp.float32, jnp.int32
    dma = pltpu.SemaphoreType.DMA
    return pl.pallas_call(
        kernel,
        out_shape=jax.ShapeDtypeStruct((ROWS, 2 * W), f32),
        in_specs=[
            pl.BlockSpec(memory_space=pltpu.SMEM),
            pl.BlockSpec(memory_space=pltpu.SMEM),
            pl.BlockSpec(memory_space=pltpu.SMEM),
            pl.BlockSpec(memory_space=pltpu.SMEM),
            pl.BlockSpec(memory_space=pl.ANY),
            pl.BlockSpec(memory_space=pl.ANY),
        ],
        out_specs=pl.BlockSpec(memory_space=pltpu.VMEM),
        scratch_shapes=[
            pltpu.VMEM((stack, W, W), bf16),
            pltpu.VMEM((ROWS, M * W), bf16),
            pltpu.VMEM((ROWS, M * W), bf16),
            pltpu.VMEM((ROWS, M * W), bf16),
            pltpu.VMEM((ROWS, M * W), bf16),
            pltpu.VMEM((NC, 2, 2, H, W), bf16),
            pltpu.VMEM((NC, 2, 2, H, W), bf16),
            pltpu.VMEM((8, 2, 2, H, W), bf16),
            pltpu.VMEM((NC, 2, W), i32),
            pltpu.VMEM((NC, 2, W), i32),
            pltpu.VMEM((8, 2, W), i32),
            pltpu.VMEM((2 * M, W // 8, 8, W), f32),
            pltpu.VMEM((2 * M, W // 8, 8, W), f32),
            pltpu.VMEM((M, 2, H, 2 * W), bf16),
            pltpu.VMEM((M, 2, H, 2 * W), bf16),
            pltpu.VMEM((M, 2, H, 2 * W), bf16),
            pltpu.VMEM((M, 2, H, 2 * W), bf16),
            dma((1 + 2 * M,)),
            dma((NC, 2)), dma((NC, 2)), dma((NC,)), dma((NC,)),
            dma((8, 2)), dma((8, 2)), dma((8,)), dma((8,)),
            dma((CHUNKS,)), dma((CHUNKS,)), dma((CHUNKS,)), dma((CHUNKS,)),
            dma((CHUNKS, 2)), dma((CHUNKS, 2)), dma((CHUNKS, 2)), dma((CHUNKS, 2)),
        ],
        compiler_params=pltpu.CompilerParams(
            collective_id=0, has_side_effects=True, vmem_limit_bytes=62 * 1024 * 1024
        ),
        cost_estimate=pl.CostEstimate(flops=2 * ROWS * 3 * M * W * 2 * W, bytes_accessed=6 << 20, transcendentals=0),
    )(low, high, margin_place, density_pattern, density_panel, margin_blocks[0])


def solution(mesh):
    return jax.shard_map(
        on_device,
        mesh=mesh,
        in_specs=(
            P("row", "col"),
            P("row", "col"),
            P("row", "col", None, None),
            P("row", "col", None),
            P("row", "col"),
        ),
        out_specs=P("row", "col"),
        check_vma=False,
    )
```

time: 107 us -> 106 us (level); the launches traced: 107 us -> 104 us
  Pallas kernels: 103 us -> 101 us
    pallas_call x1, Pallas kernels: 103 us -> 101 us  [on_device(): pl.pallas_call(kernel, out_shape=jax.ShapeDtypeStruct((ROWS, 2 * W), f32)...]
where the time goes in v4:
time: 106 us; the launch traced here: 104 us
  Pallas kernels  101 us (95%)
  local copies, waits for them, and re-layouts  1.87 us (2%)
  other arithmetic  1.37 us (1%)
    pallas_call x1, Pallas kernels, on_device(): pl.pallas_call(kernel, out_shape=jax.ShapeDtypeStruct((ROWS, 2 * W), f32)...  101 us

profile of v4, /device:TPU:6, one launch (start us, length us, event | category | flops | bytes accessed | tf_op | source)
XLA Modules:
  0.0 104.2 jit_solution(5798982695867902265)
XLA Ops:
  0.0 1.4 %select_reduce_fusion = (s32[32]{0:T(128)}, s32[32]{0:T(128)}) fusion(s32[32]{0:T(128)} %bitcast.3), kind=kLoop, calls=%fused_computation | loop fusion | flops 5056 | bytes 384 | tf_op jit(solution)/shard_map/reduce_max | solution.py:435
  1.4 101.0 %shard_map.55 = f32[512,256]{1,0:T(8,128)} custom-call(s32[32]{0:T(128)} %get-tuple-element.6.low, s32[32]{0:T(128)} %get-tuple-element.5.high, s32[1,32]{1,0:T(1,128)} %places.1, s32[4,24]{1,0:T(4,128)} %pattern.1, bf16[512,3072]{1,0:T(8,128)(2,1)} %density.1, bf16[32,128,128]{2,1,0:T(8,128)(2,1)} %bitcast.2), custom_call_target="tpu_custom_call" | custom-call | flops 805306368 | bytes 6291456 | tf_op jit(solution)/shard_map/pallas_call | solution.py:439
  102.3 1.9 %copy.7 = f32[512,256]{1,0:T(8,128)} copy(f32[512,256]{1,0:T(8,128)} %shard_map.55) | data formatting | bytes 1048576

commit v5 on v4

--- a/solution.py
+++ b/solution.py
@@ -188,8 +188,13 @@
 
     lax.fori_loop(0, 8, send_next, 0)
 
+    def send_far(e, carry):
+        first_leg(e, 1).start()
+        return carry
+
+    lax.fori_loop(0, 8, send_far, 0)
+
     def send_second(e, carry):
-        first_leg(e, 1).start()
         direct(offset_of(e, 3), 1).start()
         direct(offset_of(e, 1), 1).start()
 

time: 106 us -> 106 us (level)
  no operation moved by 1% of the time
where the time goes in v5:
time: 106 us; the launch traced here: 104 us
  Pallas kernels  101 us (95%)
  local copies, waits for them, and re-layouts  1.87 us (2%)
  other arithmetic  1.37 us (1%)
    pallas_call x1, Pallas kernels, on_device(): pl.pallas_call(kernel, out_shape=jax.ShapeDtypeStruct((ROWS, 2 * W), f32)...  101 us

profile of v5, /device:TPU:6, one launch (start us, length us, event | category | flops | bytes accessed | tf_op | source)
XLA Modules:
  0.0 104.2 jit_solution(4295165241826536511)
XLA Ops:
  0.0 1.4 %select_reduce_fusion = (s32[32]{0:T(128)}, s32[32]{0:T(128)}) fusion(s32[32]{0:T(128)} %bitcast.3), kind=kLoop, calls=%fused_computation | loop fusion | flops 5056 | bytes 384 | tf_op jit(solution)/shard_map/reduce_max | solution.py:440
  1.4 101.0 %shard_map.55 = f32[512,256]{1,0:T(8,128)} custom-call(s32[32]{0:T(128)} %get-tuple-element.6.low, s32[32]{0:T(128)} %get-tuple-element.5.high, s32[1,32]{1,0:T(1,128)} %places.1, s32[4,24]{1,0:T(4,128)} %pattern.1, bf16[512,3072]{1,0:T(8,128)(2,1)} %density.1, bf16[32,128,128]{2,1,0:T(8,128)(2,1)} %bitcast.2), custom_call_target="tpu_custom_call" | custom-call | flops 805306368 | bytes 6291456 | tf_op jit(solution)/shard_map/pallas_call | solution.py:444
  102.4 1.9 %copy.7 = f32[512,256]{1,0:T(8,128)} copy(f32[512,256]{1,0:T(8,128)} %shard_map.55) | data formatting | bytes 1048576
